TPU v7x, 256 devices: a whole 4x4x8 slice. The times are simulated.
256 devices in a mesh: bunch: 16 (over x, y), mp: 16 (over z, core).
Axes of the slice: x: 4, y: 4, z: 8, core: 2. Of those that a mesh axis runs over, the one named last changes fastest.
Arguments:
- phase_space: float32 [4, 256, 65536], P(None, 'bunch', 'mp')
- phase_advance: float32 [2, 256], P(None, 'bunch'), may hold values from 0.3 to 2.8
- centroid_history: float32 [2, 64, 256], P(None, None, 'bunch'), may hold values from -6 to 6
- lr_wake: float32 [16640], replicated, may hold values from -0.046875 to 0.046875
- sr_dipole: float32 [256, 256], replicated, may hold values from -24 to 24
- sr_quad: float32 [256, 256], replicated, may hold values from -24 to 24
- slice_ids: int32 [2, 256, 65536], P(None, 'bunch', 'mp'), may hold values from 0 to 255
Outputs:
- tracked: float32 [4, 256, 65536], P(None, 'bunch', 'mp')
- centroids: float32 [2, 2, 256], P(None, None, 'bunch')
All inputs are finite; a program needn't handle non-finite values.
Results may differ from a plain program's by a relative error of at most 0.00019.
Values sent between devices are 32-bit elements; how exact they have to be, the bound alone decides.
A program may use at most 64 MiB of HBM per device.

v0:
```python
import jax
import jax.numpy as jnp
from jax import lax
from jax.sharding import PartitionSpec as P

SLICES = 256
TURNS = 2
DETUNE = 0.02


def sent_to_all(array, axis):
    copies = jnp.broadcast_to(array, (lax.axis_size(axis), *array.shape))
    return lax.all_to_all(copies, axis, split_axis=0, concat_axis=0, tiled=True)


def over_copies(array, axis):
    everything = sent_to_all(array, axis)
    return jnp.sum(everything, axis=0)


def gather_turned(arrays, axis, dims):
    turned = [jnp.moveaxis(a, dim, 0) for a, dim in zip(arrays, dims)]
    widths = [t[0].size for t in turned]
    both = jnp.concatenate([t.reshape(-1, w) for t, w in zip(turned, widths)], axis=1)
    whole = lax.all_gather(both, axis, axis=0, tiled=True)
    tiles = jnp.split(whole, [sum(widths[:k]) for k in range(1, len(widths))], axis=1)
    return tuple(
        (
            jnp.moveaxis(b.reshape(-1, *t.shape[1:]), 0, dim)
            for b, t, dim in zip(tiles, turned, dims)
        )
    )


def body(phase_space, phase_advance, centroid_history, lr_wake, sr_dipole, sr_quad, slice_ids):
    highest = lax.Precision.HIGHEST
    bunch_dev = phase_space.shape[1]
    depth = centroid_history.shape[1]
    macro_total = phase_space.shape[2] * lax.axis_size("mp")
    all_bunches = bunch_dev * lax.axis_size("bunch")
    length = (depth + 1) * all_bunches
    offset_bunch = lax.axis_index("bunch") * bunch_dev
    own_index = jnp.arange(bunch_dev, dtype=jnp.int32)
    levels = jnp.arange(SLICES, dtype=jnp.int32)
    padded = jnp.concatenate([jnp.zeros((all_bunches,), jnp.float32), lr_wake])
    windows = jax.vmap(lambda start_at: lax.dynamic_slice(padded, (start_at,), (length,)))(
        offset_bunch + own_index
    )
    history = centroid_history

    def moments_of(member):
        slice_line, line_x, line_y = member
        onehot = (slice_line[:, None] == levels[None, :]).astype(jnp.float32)
        stacked = jnp.stack([jnp.ones_like(line_x), line_x, line_y])
        return jnp.dot(stacked, onehot, precision=highest, preferred_element_type=jnp.float32)

    def lookup(member):
        slice_line, kick_rows = member
        onehot = (slice_line[:, None] == levels[None, :]).astype(jnp.float32)
        return lax.dot_general(
            kick_rows,
            onehot,
            (((1,), (1,)), ((), ())),
            precision=highest,
            preferred_element_type=jnp.float32,
        )

    coords = phase_space
    centroid_rows = []
    for turn_index in range(TURNS):
        slice_row = slice_ids[turn_index]
        moments = lax.map(moments_of, (slice_row, coords[0], coords[2]))
        moments = over_copies(moments, "mp")
        density = moments[:, 0] / macro_total
        dipole = jnp.stack([moments[:, 1], moments[:, 2]]) / macro_total
        centroid = jnp.sum(dipole, axis=2)
        centroid_rows.append(centroid)
        dip_kick = jnp.einsum("pbj,ij->pbi", dipole, sr_dipole, precision=highest)
        quad_kick = jnp.einsum("bj,ij->bi", density, sr_quad, precision=highest)
        whole_past, current_all = gather_turned((history, centroid), "bunch", (2, 1))
        all_rows = jnp.concatenate([current_all[:, None, :], whole_past], axis=1)[
            :, :, ::-1
        ].reshape(2, length)
        far_kick = jnp.einsum("bk,pk->pb", windows, all_rows, precision=highest)
        kick_table = jnp.stack([dip_kick[0], dip_kick[1], quad_kick], axis=1)
        picked = lax.map(lookup, (slice_row, kick_table))
        coord_x, moment_x, coord_y, moment_y = (coords[0], coords[1], coords[2], coords[3])
        moment_x = moment_x + picked[:, 0] + picked[:, 2] * coord_x + far_kick[0][:, None]
        moment_y = moment_y + picked[:, 1] - picked[:, 2] * coord_y + far_kick[1][:, None]
        action = coord_x * coord_x + moment_x * moment_x + coord_y * coord_y + moment_y * moment_y
        angle_x = phase_advance[0][:, None] + DETUNE * action
        angle_y = phase_advance[1][:, None] + DETUNE * action
        new_x = jnp.cos(angle_x) * coord_x + jnp.sin(angle_x) * moment_x
        new_mx = -jnp.sin(angle_x) * coord_x + jnp.cos(angle_x) * moment_x
        new_y = jnp.cos(angle_y) * coord_y + jnp.sin(angle_y) * moment_y
        new_my = -jnp.sin(angle_y) * coord_y + jnp.cos(angle_y) * moment_y
        coords = jnp.stack([new_x, new_mx, new_y, new_my])
        history = jnp.concatenate([centroid[:, None, :], history[:, :-1]], axis=1)
    return (coords, jnp.stack(centroid_rows, axis=1))


def solution(mesh):
    placed = (
        P(None, "bunch", "mp"),
        P(None, "bunch"),
        P(None, None, "bunch"),
        P(),
        P(),
        P(),
        P(None, "bunch", "mp"),
    )
    return jax.shard_map(
        body,
        mesh=mesh,
        in_specs=placed,
        out_specs=(P(None, "bunch", "mp"), P(None, None, "bunch")),
        check_vma=False,
    )
```

profile of v0, /device:TPU:96, one launch (start us, length us, event | category | flops | bytes accessed | tf_op | source)
XLA Modules:
  0.0 322.9 jit_solution(3574766325816593291)
XLA Ops:
  1.9 25.5 %while.46 = (s32[]{:T(128)}, f32[16,3,256]{2,0,1:T(8,128)S(1)}, f32[16,4096]{1,0:T(8,128)S(1)}, f32[16,4096]{1,0:T(8,128)S(1)}, s32[16,4096]{1,0:T(8,128)S(1)}, ...) while((s32[]{:T(128)}, f32[16,3,256]{2,0,1:T(8,128)S(1)}, f32[16,4096]{1,0:T(8,128)S(1)}, ...), condition=%wide.region_1.2_spmd.clone, body=%wide.region_0.1_spmd.clone.sunk | while | flops 38821888 | bytes 162961 | solution.py:72
  2.0 1.4 fusion.77
  3.6 1.4 fusion.77
  5.2 1.4 fusion.77
  6.8 1.4 fusion.77
  8.4 1.4 fusion.77
  10.0 1.4 fusion.77
  11.6 1.4 fusion.77
  13.2 1.4 fusion.77
  14.8 1.4 fusion.77
  16.4 1.4 fusion.77
  18.0 1.4 fusion.77
  19.6 1.4 fusion.77
  21.2 1.4 fusion.77
  22.8 1.4 fusion.77
  24.4 1.4 fusion.77
  26.0 1.4 fusion.77
  28.5 7.7 %all-to-all-start = ((f32[16,16,3,256]{3,1,2,0:T(8,128)}), f32[16,16,3,256]{3,1,2,0:T(8,128)S(1)}, u32[]{:S(2)}, u32[]{:S(2)}) async-start(f32[16,16,3,256]{3,1,2,0:T(8,128)} %broadcast_in_dim.39), calls=%async_computation | async-start | bytes 1572864 | tf_op jit(solution)/shard_map/all_to_all | solution.py:13
  36.3 36.2 %while.45 = (s32[]{:T(128)}, f32[16896]{0:T(1024)S(1)}, s32[16,1]{0,1:T(1,128)S(1)}, f32[16,16640]{1,0:T(8,128)S(1)}, s32[]{:T(128)}, /*index=5*/s32[]{:T(128)}) while((s32[]{:T(128)}, f32[16896]{0:T(1024)S(1)}, s32[16,1]{0,1:T(1,128)S(1)}, f32[16,16640]{1,0:T(8,128)S(1)}, s32[]{:T(128)}, /*index=5*/s32[]{:T(128)}) %tuple.122), condition=%wide.while_cond, body=%wide.while_body.sunk | while | flops 2 | bytes 399457 | solution.py:46
  72.9 24.0 %all_gather.6 = f32[256,130]{1,0:T(8,128)S(1)} all-gather(f32[16,130]{1,0:T(8,128)S(1)} %pad_maximum_fusion.5), channel_id=1, replica_groups=mesh['bunch'=16,'mp'=16] {'bunch'}, dimensions={0}, use_global_device_ids=true | all-gather | bytes 141440 | tf_op jit(solution)/shard_map/all_gather | solution.py:25
  99.0 57.1 %while.47 = (s32[]{:T(128)}, f32[16,3,4096]{2,0,1:T(8,128)S(1)}, f32[16,3,256]{2,0,1:T(8,128)S(1)}, s32[16,4096]{1,0:T(8,128)}, s32[]{:T(128)}, /*index=5*/s32[]{:T(128)}) while((s32[]{:T(128)}, f32[16,3,4096]{2,0,1:T(8,128)S(1)}, f32[16,3,256]{2,0,1:T(8,128)S(1)}, s32[16,4096]{1,0:T(8,128)}, s32[]{:T(128)}, ...), condition=%wide.region_4.5_spmd.clone, body=%wide.region_3.4_spmd.clone.sunk | while | flops 38797312 | bytes 304217 | solution.py:86
  99.9 2.1 convolution_bitcast_fusion.6
  103.5 2.1 convolution_bitcast_fusion.6
  107.1 2.1 convolution_bitcast_fusion.6
  110.6 2.1 convolution_bitcast_fusion.6
  114.2 2.1 convolution_bitcast_fusion.6
  117.8 2.1 convolution_bitcast_fusion.6
  121.4 2.1 convolution_bitcast_fusion.6
  124.9 2.1 convolution_bitcast_fusion.6
  128.5 2.1 convolution_bitcast_fusion.6
  132.1 2.1 convolution_bitcast_fusion.6
  135.6 2.1 convolution_bitcast_fusion.6
  139.2 2.1 convolution_bitcast_fusion.6
  142.8 2.1 convolution_bitcast_fusion.6
  146.3 2.1 convolution_bitcast_fusion.6
  149.9 2.1 convolution_bitcast_fusion.6
  153.5 2.1 convolution_bitcast_fusion.6
  156.1 2.2 fusion.64
  158.4 3.0 multiply_add_fusion.5
  161.4 40.9 %while.48 = (s32[]{:T(128)}, f32[16,3,256]{2,0,1:T(8,128)S(1)}, f32[16,4096]{1,0:T(8,128)}, f32[16,4096]{1,0:T(8,128)}, s32[16,4096]{1,0:T(8,128)S(1)}, /*index=5*/s32[]{:T(128)}, f32[]{:T(128)}, f32[]{:T(128)}, s32[]{:T(128)}) while((s32[]{:T(128)}, f32[16,3,256]{2,0,1:T(8,128)S(1)}, f32[16,4096]{1,0:T(8,128)}, ...), condition=%wide.region_7.8_spmd.clone, body=%wide.region_6.7_spmd.clone.sunk | while | flops 38821888 | bytes 162961 | solution.py:72
  165.0 1.4 fusion.79
  182.9 1.4 fusion.79
  203.3 7.2 %all-to-all-start.1 = ((f32[16,16,3,256]{3,1,2,0:T(8,128)}), f32[16,16,3,256]{3,1,2,0:T(8,128)}, u32[]{:S(2)}, u32[]{:S(2)}) async-start(f32[16,16,3,256]{3,1,2,0:T(8,128)} %broadcast_in_dim.41), calls=%async_computation.1 | async-start | bytes 1572864 | tf_op jit(solution)/shard_map/all_to_all | solution.py:13
  211.8 19.5 %all-to-all-done.1 = f32[16,16,3,256]{3,1,2,0:T(8,128)} async-done(((f32[16,16,3,256]{3,1,2,0:T(8,128)}), f32[16,16,3,256]{3,1,2,0:T(8,128)}, u32[]{:S(2)}, u32[]{:S(2)}) %all-to-all-start.1) | async-done | bytes 786464 | tf_op jit(solution)/shard_map/all_to_all | solution.py:13
  232.7 23.3 %all_gather.7 = f32[256,130]{1,0:T(8,128)S(1)} all-gather(f32[16,130]{1,0:T(8,128)S(1)} %pad_maximum_fusion.6), channel_id=1, replica_groups=mesh['bunch'=16,'mp'=16] {'bunch'}, dimensions={0}, use_global_device_ids=true | all-gather | bytes 141440 | tf_op jit(solution)/shard_map/all_gather | solution.py:25
  258.7 57.1 %while.49 = (s32[]{:T(128)}, f32[16,3,4096]{2,0,1:T(8,128)S(1)}, f32[16,3,256]{2,0,1:T(8,128)S(1)}, s32[16,4096]{1,0:T(8,128)}, s32[]{:T(128)}, /*index=5*/s32[]{:T(128)}) while((s32[]{:T(128)}, f32[16,3,4096]{2,0,1:T(8,128)S(1)}, f32[16,3,256]{2,0,1:T(8,128)S(1)}, s32[16,4096]{1,0:T(8,128)}, s32[]{:T(128)}, ...), condition=%wide.region_10.11_spmd.clone, body=%wide.region_9.10_spmd.clone.sunk | while | flops 38797312 | bytes 304217 | solution.py:86
  259.7 2.1 convolution_bitcast_fusion.7
  263.2 2.1 convolution_bitcast_fusion.7
  266.8 2.1 convolution_bitcast_fusion.7
  270.4 2.1 convolution_bitcast_fusion.7
  273.9 2.1 convolution_bitcast_fusion.7
  277.5 2.1 convolution_bitcast_fusion.7
  281.1 2.1 convolution_bitcast_fusion.7
  284.7 2.1 convolution_bitcast_fusion.7
  288.2 2.1 convolution_bitcast_fusion.7
  291.8 2.1 convolution_bitcast_fusion.7
  295.4 2.1 convolution_bitcast_fusion.7
  298.9 2.1 convolution_bitcast_fusion.7
  302.5 2.1 convolution_bitcast_fusion.7
  306.1 2.1 convolution_bitcast_fusion.7
  309.6 2.1 convolution_bitcast_fusion.7
  313.2 2.1 convolution_bitcast_fusion.7
  316.4 3.2 %multiply_add_fusion.3 = (f32[1,16,4096]{2,1,0:T(8,128)S(1)}, f32[1,16,4096]{2,1,0:T(8,128)S(1)}, f32[1,16,4096]{2,1,0:T(8,128)S(1)}, f32[1,16,4096]{2,1,0:T(8,128)S(1)}, f32[1,16,4096]{2,1,0:T(8,128)S(1)}) fusion(f32[16]{0:T(128)S(1)} %get-tuple-element.282, f32[16]{0:T(128)S(1)} %get-tuple-element.280, f32[16,3,4096]{2,0,1:T(8,128)S(1)} %get-tuple-element.123, ...), kind=kLoop, calls=%fused_computation.77 | loop fusion | flops 2359296 | bytes 3408128 | tf_op jit(solution)/shard_map/add | solution.py:93
  319.7 2.2 multiply_add_fusion.1
  (447 shorter events, 132.1 us)
Async XLA Ops:
  0.6 97.9 %copy-start = (f32[256,256]{1,0:T(8,128)S(1)}, f32[256,256]{1,0:T(8,128)}, u32[]{:S(2)}) copy-start(f32[256,256]{1,0:T(8,128)} %param.19) | copy-start | bytes 786436
  0.6 1.2 copy-start.8
  27.5 1.0 copy-start.7
  27.5 8.7 %copy-start.10 = (f32[2,64,16]{1,2,0:T(8,128)S(1)}, f32[2,64,16]{1,2,0:T(8,128)}, u32[]{:S(2)}) copy-start(f32[2,64,16]{1,2,0:T(8,128)} %param.17) | copy-start | bytes 24580
  27.5 8.8 %copy-start.9 = (f32[16640]{0:T(1024)S(1)}, f32[16640]{0:T(1024)}, u32[]{:S(2)}) copy-start(f32[16640]{0:T(1024)} %param.18) | copy-start | bytes 199684
  28.5 44.1 %all-to-all-start = ((f32[16,16,3,256]{3,1,2,0:T(8,128)}), f32[16,16,3,256]{3,1,2,0:T(8,128)S(1)}, u32[]{:S(2)}, u32[]{:S(2)}) async-start(f32[16,16,3,256]{3,1,2,0:T(8,128)} %broadcast_in_dim.39), calls=%async_computation | async-start | bytes 1572864 | tf_op jit(solution)/shard_map/all_to_all | solution.py:13
  72.7 25.6 %copy-start.4 = (f32[256,256]{1,0:T(8,128)S(1)}, f32[256,256]{1,0:T(8,128)}, u32[]{:S(2)}) copy-start(f32[256,256]{1,0:T(8,128)} %param.20) | copy-start | bytes 786436
  156.1 2.3 copy-start.11
  156.1 2.3 copy-start.1
  202.3 1.0 copy-start.6
  203.3 28.0 %all-to-all-start.1 = ((f32[16,16,3,256]{3,1,2,0:T(8,128)}), f32[16,16,3,256]{3,1,2,0:T(8,128)}, u32[]{:S(2)}, u32[]{:S(2)}) async-start(f32[16,16,3,256]{3,1,2,0:T(8,128)} %broadcast_in_dim.41), calls=%async_computation.1 | async-start | bytes 1572864 | tf_op jit(solution)/shard_map/all_to_all | solution.py:13
  211.8 44.2 %copy-start.5 = (f32[256,256]{1,0:T(8,128)S(1)}, f32[256,256]{1,0:T(8,128)}, u32[]{:S(2)}) copy-start(f32[256,256]{1,0:T(8,128)} %param.20) | copy-start | bytes 786436
  258.6 57.8 %copy-start.2 = (f32[1,16,4096]{2,1,0:T(8,128)S(1)}, f32[1,16,4096]{2,1,0:T(8,128)}, u32[]{:S(2)}) copy-start(f32[1,16,4096]{2,1,0:T(8,128)} %get-tuple-element.256) | copy-start | bytes 786436
  258.7 57.8 %copy-start.3 = (f32[1,16,4096]{2,1,0:T(8,128)S(1)}, f32[1,16,4096]{2,1,0:T(8,128)}, u32[]{:S(2)}) copy-start(f32[1,16,4096]{2,1,0:T(8,128)} %get-tuple-element.257) | copy-start | bytes 786436
where the time goes:
time: 324 us; the launch traced here: 323 us
  matrix products  119 us (37%)
  local copies, waits for them, and re-layouts  106 us (33%)
  blocking collectives  47.3 us (15%)
  waiting for transfers between devices  19.5 us (6%)
  starting transfers between devices  14.9 us (5%)
  other arithmetic  12.1 us (4%)
  loops' own time  3.33 us (1%)
    dot_general x32, matrix products, lookup(): lax.dot_general(kick_rows, onehot, (((1,), (1,)), ((), ())), precision=hi...  68 us
    all_gather x2, blocking collectives, gather_turned(): whole = lax.all_gather(both, axis, axis=0, tiled=True)  47.3 us
    dynamic_slice x96, local copies, waits for them, and re-layouts, body(): moments = lax.map(moments_of, (slice_row, coords[0], coords[2]))  46.7 us
    dot_general x32, matrix products, moments_of(): jnp.dot(stacked, onehot, precision=highest, preferred_element_type=jnp.fl...  46.3 us
    gather x64, local copies, waits for them, and re-layouts  35.7 us
    all_to_all x2, waiting for transfers between devices, sent_to_all(): return lax.all_to_all(copies, axis, split_axis=0, concat_axis=0, tiled=True)  19.5 us
    all_to_all x2, starting transfers between devices, sent_to_all(): return lax.all_to_all(copies, axis, split_axis=0, concat_axis=0, tiled=True)  14.9 us
    dynamic_update_slice x64, local copies, waits for them, and re-layouts, body(): picked = lax.map(lookup, (slice_row, kick_table))  14.9 us
  transfers between devices with their start and end apart: 2, of which 1 were waited for; matrix products, arithmetic and copies ran while one was open for 11% of the time, Pallas kernels for 0%

commit v1 on v0

--- a/solution.py
+++ b/solution.py
@@ -22,7 +22,9 @@
     turned = [jnp.moveaxis(a, dim, 0) for a, dim in zip(arrays, dims)]
     widths = [t[0].size for t in turned]
     both = jnp.concatenate([t.reshape(-1, w) for t, w in zip(turned, widths)], axis=1)
-    whole = lax.all_gather(both, axis, axis=0, tiled=True)
+    whole = jnp.concatenate(
+        lax.all_to_all(jnp.stack([both] * lax.axis_size(axis)), axis, 0, 0), axis=0
+    )
     tiles = jnp.split(whole, [sum(widths[:k]) for k in range(1, len(widths))], axis=1)
     return tuple(
         (

time: 324 us -> 313 us (0.966); the launches traced: 323 us -> 307 us
  blocking collectives: 47.3 us -> 0 us
  starting transfers between devices: 14.9 us -> 29.2 us
  local copies, waits for them, and re-layouts: 106 us -> 120 us
    all_gather x2 -> x0, blocking collectives: 47.3 us -> none  [gather_turned(): whole = lax.all_gather(both, axis, axis=0, tiled=True)]
    all_to_all x0 -> x2, starting transfers between devices: none -> 14.3 us  [gather_turned(): lax.all_to_all(jnp.stack([both] * lax.axis_size(axis)), axis, 0, 0)]
    rev x2, local copies, waits for them, and re-layouts: 0.67 us -> 5.84 us  [body(): jnp.concatenate([current_all[:, None, :], whole_past], axis=1)[:, :, ::-1]]
  transfers between devices with their start and end apart: 2 -> 4, of which waited for: 1 -> 1; matrix products, arithmetic and copies ran while one was open for 11% -> 49% of each run, Pallas kernels for 0% -> 0%
where the time goes in v1:
time: 313 us; the launch traced here: 307 us
  local copies, waits for them, and re-layouts  120 us (38%)
  matrix products  119 us (38%)
  starting transfers between devices  29.2 us (9%)
  waiting for transfers between devices  19.5 us (6%)
  other arithmetic  15.2 us (5%)
  loops' own time  3.35 us (1%)
    dot_general x32, matrix products, lookup(): lax.dot_general(kick_rows, onehot, (((1,), (1,)), ((), ())), precision=hi...  68 us
    dynamic_slice x96, local copies, waits for them, and re-layouts, body(): moments = lax.map(moments_of, (slice_row, coords[0], coords[2]))  46.6 us
    dot_general x32, matrix products, moments_of(): jnp.dot(stacked, onehot, precision=highest, preferred_element_type=jnp.fl...  46.3 us
    gather x64, local copies, waits for them, and re-layouts  36.1 us
    all_to_all x2, waiting for transfers between devices, sent_to_all(): return lax.all_to_all(copies, axis, split_axis=0, concat_axis=0, tiled=True)  19.5 us
    all_to_all x2, starting transfers between devices, sent_to_all(): return lax.all_to_all(copies, axis, split_axis=0, concat_axis=0, tiled=True)  14.9 us
    dynamic_update_slice x64, local copies, waits for them, and re-layouts, body(): picked = lax.map(lookup, (slice_row, kick_table))  14.9 us
    all_to_all x2, starting transfers between devices, gather_turned(): lax.all_to_all(jnp.stack([both] * lax.axis_size(axis)), axis, 0, 0)  14.3 us
  transfers between devices with their start and end apart: 4, of which 1 were waited for; matrix products, arithmetic and copies ran while one was open for 49% of the time, Pallas kernels for 0%

profile of v1, /device:TPU:96, one launch (start us, length us, event | category | flops | bytes accessed | tf_op | source)
XLA Modules:
  0.0 307.0 jit_solution(11033215823786602442)
XLA Ops:
  1.9 25.5 %while.46 = (s32[]{:T(128)}, f32[16,3,256]{2,0,1:T(8,128)S(1)}, f32[16,4096]{1,0:T(8,128)S(1)}, f32[16,4096]{1,0:T(8,128)S(1)}, s32[16,4096]{1,0:T(8,128)S(1)}, ...) while((s32[]{:T(128)}, f32[16,3,256]{2,0,1:T(8,128)S(1)}, f32[16,4096]{1,0:T(8,128)S(1)}, ...), condition=%wide.region_1.2_spmd.clone, body=%wide.region_0.1_spmd.clone.sunk | while | flops 38821888 | bytes 162961 | solution.py:74
  2.0 1.4 fusion.77
  3.6 1.4 fusion.77
  5.2 1.4 fusion.77
  6.8 1.4 fusion.77
  8.4 1.4 fusion.77
  10.0 1.4 fusion.77
  11.6 1.4 fusion.77
  13.2 1.4 fusion.77
  14.8 1.4 fusion.77
  16.4 1.4 fusion.77
  18.0 1.4 fusion.77
  19.6 1.4 fusion.77
  28.5 7.7 %all-to-all-start = ((f32[16,16,3,256]{3,1,2,0:T(8,128)}), f32[16,16,3,256]{3,1,2,0:T(8,128)S(1)}, u32[]{:S(2)}, u32[]{:S(2)}) async-start(f32[16,16,3,256]{3,1,2,0:T(8,128)} %broadcast_in_dim.39), calls=%async_computation | async-start | bytes 1572864 | tf_op jit(solution)/shard_map/all_to_all | solution.py:13
  36.3 36.6 %while.45 = (s32[]{:T(128)}, f32[16896]{0:T(1024)S(1)}, s32[16,1]{0,1:T(1,128)S(1)}, f32[16,16640]{1,0:T(8,128)S(1)}, s32[]{:T(128)}, /*index=5*/s32[]{:T(128)}) while((s32[]{:T(128)}, f32[16896]{0:T(1024)S(1)}, s32[16,1]{0,1:T(1,128)S(1)}, f32[16,16640]{1,0:T(8,128)S(1)}, s32[]{:T(128)}, /*index=5*/s32[]{:T(128)}) %tuple.125), condition=%wide.while_cond, body=%wide.while_body.sunk | while | flops 2 | bytes 399457 | solution.py:48
  74.0 7.0 %all-to-all-start.1 = ((f32[16,16,130]{2,1,0:T(8,128)}), f32[16,16,130]{2,1,0:T(8,128)S(1)}, u32[]{:S(2)}, u32[]{:S(2)}) async-start(f32[16,16,130]{2,1,0:T(8,128)} %stack.35), calls=%async_computation.1 | async-start | bytes 524288 | tf_op jit(solution)/shard_map/all_to_all | solution.py:26
  81.8 57.1 %while.47 = (s32[]{:T(128)}, f32[16,3,4096]{2,0,1:T(8,128)S(1)}, f32[16,3,256]{2,0,1:T(8,128)S(1)}, s32[16,4096]{1,0:T(8,128)}, s32[]{:T(128)}, /*index=5*/s32[]{:T(128)}) while((s32[]{:T(128)}, f32[16,3,4096]{2,0,1:T(8,128)S(1)}, f32[16,3,256]{2,0,1:T(8,128)S(1)}, s32[16,4096]{1,0:T(8,128)}, s32[]{:T(128)}, ...), condition=%wide.region_4.5_spmd.clone, body=%wide.region_3.4_spmd.clone.sunk | while | flops 38797312 | bytes 304217 | solution.py:88
  82.8 2.1 convolution_bitcast_fusion.6
  86.3 2.1 convolution_bitcast_fusion.6
  89.9 2.1 convolution_bitcast_fusion.6
  93.5 2.1 convolution_bitcast_fusion.6
  97.0 2.1 convolution_bitcast_fusion.6
  100.6 2.1 convolution_bitcast_fusion.6
  104.2 2.1 convolution_bitcast_fusion.6
  107.7 2.1 convolution_bitcast_fusion.6
  111.3 2.1 convolution_bitcast_fusion.6
  114.9 2.1 convolution_bitcast_fusion.6
  118.4 2.1 convolution_bitcast_fusion.6
  122.0 2.1 convolution_bitcast_fusion.6
  125.6 2.1 convolution_bitcast_fusion.6
  129.1 2.1 convolution_bitcast_fusion.6
  132.7 2.1 convolution_bitcast_fusion.6
  136.3 2.1 convolution_bitcast_fusion.6
  141.2 2.9 rev.6
  147.1 3.1 multiply_add_fusion.5
  150.2 40.9 %while.48 = (s32[]{:T(128)}, f32[16,3,256]{2,0,1:T(8,128)S(1)}, f32[16,4096]{1,0:T(8,128)}, f32[16,4096]{1,0:T(8,128)}, s32[16,4096]{1,0:T(8,128)S(1)}, /*index=5*/s32[]{:T(128)}, f32[]{:T(128)}, f32[]{:T(128)}, s32[]{:T(128)}) while((s32[]{:T(128)}, f32[16,3,256]{2,0,1:T(8,128)S(1)}, f32[16,4096]{1,0:T(8,128)}, ...), condition=%wide.region_7.8_spmd.clone, body=%wide.region_6.7_spmd.clone.sunk | while | flops 38821888 | bytes 162961 | solution.py:74
  169.1 1.4 fusion.79
  187.0 1.4 fusion.79
  192.1 7.2 %all-to-all-start.2 = ((f32[16,16,3,256]{3,1,2,0:T(8,128)}), f32[16,16,3,256]{3,1,2,0:T(8,128)}, u32[]{:S(2)}, u32[]{:S(2)}) async-start(f32[16,16,3,256]{3,1,2,0:T(8,128)} %broadcast_in_dim.41), calls=%async_computation.2 | async-start | bytes 1572864 | tf_op jit(solution)/shard_map/all_to_all | solution.py:13
  200.6 19.5 %all-to-all-done.2 = f32[16,16,3,256]{3,1,2,0:T(8,128)} async-done(((f32[16,16,3,256]{3,1,2,0:T(8,128)}), f32[16,16,3,256]{3,1,2,0:T(8,128)}, u32[]{:S(2)}, u32[]{:S(2)}) %all-to-all-start.2) | async-done | bytes 786464 | tf_op jit(solution)/shard_map/all_to_all | solution.py:13
  223.8 7.3 %all-to-all-start.3 = ((f32[16,16,130]{2,1,0:T(8,128)}), f32[16,16,130]{2,1,0:T(8,128)}, u32[]{:S(2)}, u32[]{:S(2)}) async-start(f32[16,16,130]{2,1,0:T(8,128)} %stack.39), calls=%async_computation.3 | async-start | bytes 524288 | tf_op jit(solution)/shard_map/all_to_all | solution.py:26
  231.2 57.1 %while.49 = (s32[]{:T(128)}, f32[16,3,4096]{2,0,1:T(8,128)S(1)}, f32[16,3,256]{2,0,1:T(8,128)S(1)}, s32[16,4096]{1,0:T(8,128)}, s32[]{:T(128)}, /*index=5*/s32[]{:T(128)}) while((s32[]{:T(128)}, f32[16,3,4096]{2,0,1:T(8,128)S(1)}, f32[16,3,256]{2,0,1:T(8,128)S(1)}, s32[16,4096]{1,0:T(8,128)}, s32[]{:T(128)}, ...), condition=%wide.region_10.11_spmd.clone, body=%wide.region_9.10_spmd.clone.sunk | while | flops 38797312 | bytes 304217 | solution.py:88
  232.1 2.1 convolution_bitcast_fusion.7
  235.7 2.1 convolution_bitcast_fusion.7
  239.3 2.1 convolution_bitcast_fusion.7
  242.8 2.1 convolution_bitcast_fusion.7
  246.4 2.1 convolution_bitcast_fusion.7
  250.0 2.1 convolution_bitcast_fusion.7
  253.5 2.1 convolution_bitcast_fusion.7
  257.1 2.1 convolution_bitcast_fusion.7
  260.7 2.1 convolution_bitcast_fusion.7
  264.3 2.1 convolution_bitcast_fusion.7
  267.8 2.1 convolution_bitcast_fusion.7
  271.4 2.1 convolution_bitcast_fusion.7
  275.0 2.1 convolution_bitcast_fusion.7
  278.5 2.1 convolution_bitcast_fusion.7
  282.1 2.1 convolution_bitcast_fusion.7
  285.7 2.1 convolution_bitcast_fusion.7
  288.9 1.6 split.19
  291.4 1.7 copy.73
  293.7 1.6 pad_maximum_fusion.2
  295.3 2.9 rev.7
  300.5 3.3 %multiply_add_fusion.3 = (f32[1,16,4096]{2,1,0:T(8,128)S(1)}, f32[1,16,4096]{2,1,0:T(8,128)S(1)}, f32[1,16,4096]{2,1,0:T(8,128)S(1)}, f32[1,16,4096]{2,1,0:T(8,128)S(1)}, f32[1,16,4096]{2,1,0:T(8,128)S(1)}) fusion(f32[16]{0:T(128)S(1)} %copy-done.16, f32[16]{0:T(128)S(1)} %get-tuple-element.290, f32[16,3,4096]{2,0,1:T(8,128)S(1)} %get-tuple-element.123, ...), kind=kLoop, calls=%fused_computation.77 | loop fusion | flops 2359296 | bytes 3408128 | tf_op jit(solution)/shard_map/add | solution.py:95
  303.8 2.2 multiply_add_fusion.1
  (461 shorter events, 146.5 us)
Async XLA Ops:
  0.6 80.7 %copy-start = (f32[256,256]{1,0:T(8,128)S(1)}, f32[256,256]{1,0:T(8,128)}, u32[]{:S(2)}) copy-start(f32[256,256]{1,0:T(8,128)} %param.19) | copy-start | bytes 786436
  0.6 1.2 copy-start.7
  27.5 1.0 copy-start.6
  27.5 8.7 %copy-start.9 = (f32[2,64,16]{1,2,0:T(8,128)S(1)}, f32[2,64,16]{1,2,0:T(8,128)}, u32[]{:S(2)}) copy-start(f32[2,64,16]{1,2,0:T(8,128)} %param.17) | copy-start | bytes 24580
  27.5 8.8 %copy-start.8 = (f32[16640]{0:T(1024)S(1)}, f32[16640]{0:T(1024)}, u32[]{:S(2)}) copy-start(f32[16640]{0:T(1024)} %param.18) | copy-start | bytes 199684
  28.5 44.5 %all-to-all-start = ((f32[16,16,3,256]{3,1,2,0:T(8,128)}), f32[16,16,3,256]{3,1,2,0:T(8,128)S(1)}, u32[]{:S(2)}, u32[]{:S(2)}) async-start(f32[16,16,3,256]{3,1,2,0:T(8,128)} %broadcast_in_dim.39), calls=%async_computation | async-start | bytes 1572864 | tf_op jit(solution)/shard_map/all_to_all | solution.py:13
  73.0 8.1 %copy-start.4 = (f32[256,256]{1,0:T(8,128)S(1)}, f32[256,256]{1,0:T(8,128)}, u32[]{:S(2)}) copy-start(f32[256,256]{1,0:T(8,128)} %param.20) | copy-start | bytes 786436
  73.1 0.8 copy-start.11
  74.0 64.9 %all-to-all-start.1 = ((f32[16,16,130]{2,1,0:T(8,128)}), f32[16,16,130]{2,1,0:T(8,128)S(1)}, u32[]{:S(2)}, u32[]{:S(2)}) async-start(f32[16,16,130]{2,1,0:T(8,128)} %stack.35), calls=%async_computation.1 | async-start | bytes 524288 | tf_op jit(solution)/shard_map/all_to_all | solution.py:26
  139.7 7.4 %copy-start.1 = (f32[4,16,4096]{2,1,0:T(8,128)S(1)}, f32[4,16,4096]{2,1,0:T(8,128)}, u32[]{:S(2)}) copy-start(f32[4,16,4096]{2,1,0:T(8,128)} %param.15) | copy-start | bytes 3145732
  147.1 3.1 %copy-start.13 = (f32[16]{0:T(128)}, f32[16]{0:T(128)S(1)}, u32[]{:S(2)}) copy-start(f32[16]{0:T(128)S(1)} %get-tuple-element.291) | copy-start | bytes 196
  147.1 3.1 %copy-start.15 = (f32[16]{0:T(128)}, f32[16]{0:T(128)S(1)}, u32[]{:S(2)}) copy-start(f32[16]{0:T(128)S(1)} %get-tuple-element.292) | copy-start | bytes 196
  191.1 1.0 copy-start.5
  191.1 8.2 %copy-start.12 = (f32[2,16]{1,0:T(2,128)S(1)}, f32[2,16]{1,0:T(2,128)}, u32[]{:S(2)}) copy-start(f32[2,16]{1,0:T(2,128)} %copy-done.11) | copy-start | bytes 388
  191.1 8.3 %copy-start.10 = (f32[2,64,16]{1,2,0:T(8,128)S(1)}, f32[2,64,16]{1,2,0:T(8,128)}, u32[]{:S(2)}) copy-start(f32[2,64,16]{1,2,0:T(8,128)} %param.17) | copy-start | bytes 24580
  192.1 28.0 %all-to-all-start.2 = ((f32[16,16,3,256]{3,1,2,0:T(8,128)}), f32[16,16,3,256]{3,1,2,0:T(8,128)}, u32[]{:S(2)}, u32[]{:S(2)}) async-start(f32[16,16,3,256]{3,1,2,0:T(8,128)} %broadcast_in_dim.41), calls=%async_computation.2 | async-start | bytes 1572864 | tf_op jit(solution)/shard_map/all_to_all | solution.py:13
  223.8 65.1 %all-to-all-start.3 = ((f32[16,16,130]{2,1,0:T(8,128)}), f32[16,16,130]{2,1,0:T(8,128)}, u32[]{:S(2)}, u32[]{:S(2)}) async-start(f32[16,16,130]{2,1,0:T(8,128)} %stack.39), calls=%async_computation.3 | async-start | bytes 524288 | tf_op jit(solution)/shard_map/all_to_all | solution.py:26
  293.7 6.8 %copy-start.14 = (f32[16]{0:T(128)S(1)}, f32[16]{0:T(128)}, u32[]{:S(2)}) copy-start(f32[16]{0:T(128)} %copy-done.13) | copy-start | bytes 196
  293.7 6.8 %copy-start.16 = (f32[16]{0:T(128)S(1)}, f32[16]{0:T(128)}, u32[]{:S(2)}) copy-start(f32[16]{0:T(128)} %copy-done.15) | copy-start | bytes 196
  298.2 2.3 copy-start.2
  298.2 2.3 copy-start.3
